TPU v7x, 512 devices: a whole 4x8x8 slice. The times are simulated.
512 devices in a mesh: row: 16 (over x_hi, z), col: 32 (over y, x_lo, core).
Axes of the slice: x: 4 (x_hi: 2, x_lo: 2; x = x_hi * 2 + x_lo), y: 8, z: 8, core: 2. Of those that a mesh axis runs over, the one named last changes fastest.
Arguments:
- tokens: bfloat16 [256, 8192], P('col', 'row'), may hold values from -6 to 6
- upstream: bfloat16 [256, 8192], P('col', 'row'), may hold values from -6 to 6
- gate_pre: bfloat16 [256, 24576], P('row', 'col'), may hold values from -6 to 6
- up_pre: bfloat16 [256, 24576], P('row', 'col'), may hold values from -6 to 6
- w_gate: bfloat16 [8192, 24576], P('row', 'col'), may hold values from -0.0625 to 0.0625
- w_up: bfloat16 [8192, 24576], P('row', 'col'), may hold values from -0.0625 to 0.0625
- w_down: bfloat16 [24576, 8192], P('col', 'row'), may hold values from -0.0625 to 0.0625
Outputs:
- input_grad: bfloat16 [256, 8192], P('col', 'row')
- gate_grad: bfloat16 [8192, 24576], P('row', 'col')
- up_grad: bfloat16 [8192, 24576], P('row', 'col')
- down_grad: bfloat16 [24576, 8192], P('col', 'row')
All inputs are finite; a program needn't handle non-finite values.
Results may differ from a plain program's by a relative error of at most 0.0049.
Values may be sent and summed in bfloat16 or wider, within the bound.
A program may use at most 64 MiB of HBM per device.

v0:
```python
import jax
import jax.numpy as jnp
from jax import lax
from jax.sharding import PartitionSpec as P


def local_deltas(hidden_grad, gate_pre, up_pre):
    gate_value = gate_pre.astype(jnp.float32)
    up_value = up_pre.astype(jnp.float32)
    sigmoid_gate = jax.nn.sigmoid(gate_value)
    activated = gate_value * sigmoid_gate
    hidden = (activated * up_value).astype(jnp.bfloat16)
    up_delta = (hidden_grad * activated).astype(jnp.bfloat16)
    slope = sigmoid_gate * (1.0 + gate_value * (1.0 - sigmoid_gate))
    gate_delta = (hidden_grad * up_value * slope).astype(jnp.bfloat16)
    return (gate_delta, up_delta, hidden)


def on_device(tokens, upstream, gate_pre, up_pre, w_gate, w_up, w_down):
    upstream_all = lax.all_gather(upstream, "col", axis=0, tiled=True)
    total_tokens = upstream_all.shape[0]
    contract_last = (((1,), (1,)), ((), ()))
    contract_first = (((0,), (0,)), ((), ()))
    block_rows = upstream_all
    hidden_grad = lax.psum_scatter(
        lax.dot_general(block_rows, w_down, contract_last, preferred_element_type=jnp.float32),
        "row",
        scatter_dimension=0,
        tiled=True,
    )
    gate_delta, up_delta, hidden = local_deltas(hidden_grad, gate_pre, up_pre)
    gate_all, up_all, hidden_all = (
        lax.all_gather(gate_delta, "row", axis=0, tiled=True),
        lax.all_gather(up_delta, "row", axis=0, tiled=True),
        lax.all_gather(hidden, "row", axis=0, tiled=True),
    )
    gate_rows_part = gate_all
    up_rows_part = up_all
    input_grad = lax.psum_scatter(
        lax.dot_general(gate_rows_part, w_gate, contract_last, preferred_element_type=jnp.float32)
        + lax.dot_general(up_rows_part, w_up, contract_last, preferred_element_type=jnp.float32),
        "col",
        scatter_dimension=0,
        tiled=True,
    ).astype(jnp.bfloat16)
    grad_scale = float(total_tokens) ** (-0.5)
    block_rows = lax.all_gather(tokens, "col", axis=0, tiled=True)
    gate_rows_part = gate_all
    up_rows_part = up_all
    gate_total = lax.dot_general(
        block_rows, gate_rows_part, contract_first, preferred_element_type=jnp.float32
    )
    up_total = lax.dot_general(
        block_rows, up_rows_part, contract_first, preferred_element_type=jnp.float32
    )
    gate_grad = (gate_total * grad_scale).astype(jnp.bfloat16)
    up_grad = (up_total * grad_scale).astype(jnp.bfloat16)
    down_sum = lax.dot_general(
        hidden_all, upstream_all, contract_first, preferred_element_type=jnp.float32
    )
    down_grad = (down_sum * grad_scale).astype(jnp.bfloat16)
    return (input_grad, gate_grad, up_grad, down_grad)


def solution(mesh):
    placed = (
        P("col", "row"),
        P("col", "row"),
        P("row", "col"),
        P("row", "col"),
        P("row", "col"),
        P("row", "col"),
        P("col", "row"),
    )
    return jax.shard_map(
        on_device,
        mesh=mesh,
        in_specs=placed,
        out_specs=(P("col", "row"), P("row", "col"), P("row", "col"), P("col", "row")),
        check_vma=False,
    )
```

profile of v0, /device:TPU:7, one launch (start us, length us, event | category | flops | bytes accessed | tf_op | source)
XLA Modules:
  0.0 452.1 jit_solution(16449113848229801316)
XLA Ops:
  7.2 0.0 copy-start
  7.2 0.0 reduce-scatter.3.cloned.1.call-start
  7.2 33.6 %all_gather.15 = bf16[256,512]{1,0:T(8,128)(2,1)S(1)} all-gather(bf16[8,512]{1,0:T(8,128)(2,1)} %param.8), channel_id=1, replica_groups=mesh['row'=16,'col'=32] {'col'}, dimensions={0}, use_global_device_ids=true | all-gather | bytes 270336 | tf_op jit(solution)/shard_map/all_gather | solution.py:20
  40.8 0.0 copy-done
  40.8 1.3 fusion.10
  42.1 0.0 copy-start.3
  42.1 0.0 copy-start.4
  42.1 0.0 copy-start.2
  42.1 0.0 reduce-scatter.3.cloned.1.call-update
  42.2 0.0 reduce-scatter.5.cloned.1.call-start
  42.2 206.0 %reduce-scatter.3.cloned.1.call-done = f32[16,768]{1,0:T(8,128)} async-done(((f32[256,768]{1,0:T(8,128)}), f32[16,768]{1,0:T(8,128)}) %reduce-scatter.3.cloned.1.call-update) | async-done | bytes 49168 | tf_op jit(solution)/shard_map/reduce_scatter | solution.py:25
  248.2 0.0 copy-done.3
  248.2 0.0 copy-done.4
  248.3 0.8 multiply_convert_fusion.3
  249.1 33.6 %all_gather.16 = bf16[256,768]{1,0:T(8,128)(2,1)S(1)} all-gather(bf16[16,768]{1,0:T(8,128)(2,1)S(1)} %get-tuple-element.9), channel_id=1, replica_groups=mesh['row'=16,'col'=32] {'row'}, dimensions={0}, use_global_device_ids=true | all-gather | bytes 417792 | tf_op jit(solution)/shard_map/all_gather | solution.py:33
  282.7 31.2 %all_gather.17 = bf16[256,768]{1,0:T(8,128)(2,1)S(1)} all-gather(bf16[16,768]{1,0:T(8,128)(2,1)S(1)} %get-tuple-element.8), channel_id=1, replica_groups=mesh['row'=16,'col'=32] {'row'}, dimensions={0}, use_global_device_ids=true | all-gather | bytes 417792 | tf_op jit(solution)/shard_map/all_gather | solution.py:34
  313.9 0.0 copy-done.2
  313.9 0.0 copy-start.1
  313.9 0.4 fusion.11
  314.3 0.7 copy-done.1
  315.0 0.0 copy-start.5
  315.0 1.2 convolution_add_fusion
  316.2 0.0 reduce-scatter.5.cloned.1.call-update
  316.3 0.0 copy-done.5
  316.3 51.8 %all_gather.18 = bf16[256,512]{1,0:T(8,128)(2,1)S(1)} all-gather(bf16[8,512]{1,0:T(8,128)(2,1)S(1)} %copy-done.5), channel_id=1, replica_groups=mesh['row'=16,'col'=32] {'col'}, dimensions={0}, use_global_device_ids=true | all-gather | bytes 270336 | tf_op jit(solution)/shard_map/all_gather | solution.py:47
  368.1 0.4 fusion
  368.5 1.2 copy.11
  369.6 0.4 fusion.1
  370.0 1.2 copy.12
  371.2 33.2 %all_gather.19 = bf16[256,768]{1,0:T(8,128)(2,1)S(1)} all-gather(bf16[16,768]{1,0:T(8,128)(2,1)S(1)} %get-tuple-element.10), channel_id=1, replica_groups=mesh['row'=16,'col'=32] {'row'}, dimensions={0}, use_global_device_ids=true | all-gather | bytes 417792 | tf_op jit(solution)/shard_map/all_gather | solution.py:35
  404.4 1.3 multiply_convert_fusion
  405.7 38.2 %reduce-scatter.5.cloned.1.call-done = f32[8,512]{1,0:T(8,128)} async-done(((f32[256,512]{1,0:T(8,128)}), f32[8,512]{1,0:T(8,128)}) %reduce-scatter.5.cloned.1.call-update) | async-done | bytes 16400 | tf_op jit(solution)/shard_map/reduce_scatter | solution.py:39
  443.9 1.3 convert_element_type.37
Async XLA Ops:
  7.2 33.7 %copy-start = (bf16[768,512]{1,0:T(8,128)(2,1)S(1)}, bf16[768,512]{1,0:T(8,128)(2,1)}, u32[]{:S(2)}) copy-start(bf16[768,512]{1,0:T(8,128)(2,1)} %param.13) | copy-start | bytes 2359300
  7.2 241.1 %reduce-scatter.3.cloned.1.call-start = ((), (), s32[]{:S(2)}) async-start(), calls=%async_computation.2 | async-start | bytes 835584 | tf_op jit(solution)/shard_map/reduce_scatter | solution.py:25
  42.1 206.1 %copy-start.3 = (bf16[16,768]{1,0:T(8,128)(2,1)S(1)}, bf16[16,768]{1,0:T(8,128)(2,1)}, u32[]{:S(2)}) copy-start(bf16[16,768]{1,0:T(8,128)(2,1)} %param.9) | copy-start | bytes 73732
  42.1 206.1 %copy-start.4 = (bf16[16,768]{1,0:T(8,128)(2,1)S(1)}, bf16[16,768]{1,0:T(8,128)(2,1)}, u32[]{:S(2)}) copy-start(bf16[16,768]{1,0:T(8,128)(2,1)} %param.10) | copy-start | bytes 73732
  42.1 271.8 %copy-start.2 = (bf16[512,768]{1,0:T(8,128)(2,1)S(1)}, bf16[512,768]{1,0:T(8,128)(2,1)}, u32[]{:S(2)}) copy-start(bf16[512,768]{1,0:T(8,128)(2,1)} %param.11) | copy-start | bytes 2359300
  42.2 401.7 %reduce-scatter.5.cloned.1.call-start = ((), (), s32[]{:S(2)}) async-start(), calls=%async_computation.3 | async-start | bytes 540672 | tf_op jit(solution)/shard_map/reduce_scatter | solution.py:39
  313.9 1.1 copy-start.1
  315.0 1.2 copy-start.5
Sparse Core Ops, SparseCore 0:
  42.3 205.9 reduce-scatter.2
  316.4 127.4 reduce-scatter.4
where the time goes:
time: 459 us; the launch traced here: 452 us
  waiting for transfers between devices  244 us (53%)
  blocking collectives  183 us (40%)
  between operations  14.1 us (3%)
  matrix products  4.93 us (1%)
    reduce_scatter x1, waiting for transfers between devices, on_device(): lax.psum_scatter(lax.dot_general(block_rows, w_down, contract_last, prefe...  206 us
    all_gather x1, blocking collectives, on_device(): block_rows = lax.all_gather(tokens, 'col', axis=0, tiled=True)  51.8 us
    reduce_scatter x1, waiting for transfers between devices, on_device(): lax.psum_scatter(lax.dot_general(gate_rows_part, w_gate, contract_last, p...  38.2 us
    all_gather x1, blocking collectives, on_device(): lax.all_gather(gate_delta, 'row', axis=0, tiled=True)  33.6 us
    all_gather x1, blocking collectives, on_device(): upstream_all = lax.all_gather(upstream, 'col', axis=0, tiled=True)  33.6 us
    all_gather x1, blocking collectives, on_device(): lax.all_gather(hidden, 'row', axis=0, tiled=True)  33.2 us
    all_gather x1, blocking collectives, on_device(): lax.all_gather(up_delta, 'row', axis=0, tiled=True)  31.2 us
  transfers between devices with their start and end apart: 2, of which 2 were waited for; matrix products, arithmetic and copies ran while one was open for 1% of the time, Pallas kernels for 0%

commit v1 on v0

v1 whole, which is shorter than its diff:
```python
import functools

import jax
import jax.numpy as jnp
from jax import lax
from jax.experimental import pallas as pl
from jax.experimental.pallas import tpu as pltpu
from jax.sharding import PartitionSpec as P

MESH = pl.DeviceIdType.MESH
F32 = jnp.float32
BF16 = jnp.bfloat16
LAST = (((1,), (1,)), ((), ()))
FIRST = (((0,), (0,)), ((), ()))


def far_first(n):
    return sorted(range(1, n), key=lambda d: (-min(d, n - d), d))


def near_first(n):
    return sorted(range(1, n), key=lambda d: (min(d, n - d), d))


def exchange(
    n,
    ups, tok, gate, upre, w_gate, w_up, w_down,
    ig_out, gd_out, ud_out, hid_out, tok_out, ups_out,
    wg, wu, wd, ups_buf, tok_buf, gp_buf, up_buf, own_part, x_send, x_recv, z_send, z_recv,
    hg_buf, act, slope_up, ig_part, core_recv, xl_send, xl_recv, y_send, y_recv,
    local_sem, send_sem, ups_sem, tok_sem, gp_sem, up_sem, half_sem, quad_sem,
    xr_sem, zr_sem, hz_sem, hx_sem, ig_sem, ig_y_sem,
):
    row, col = lax.axis_index("row"), lax.axis_index("col")
    xh, z = row // n, lax.rem(row, n)
    y, q = col // 4, lax.rem(col, 4)
    xl, co = q // 2, lax.rem(q, 2)
    other = 1 - xh

    def z_peer(d):
        return (xh * n + lax.rem(z + d, n), col)

    def y_peer(d):
        return (row, lax.rem(y + d, n) * 4 + q)

    xh_peer = (other * n + z, col)
    xl_peer = (row, y * 4 + (1 - xl) * 2 + co)
    co_peer = (row, y * 4 + xl * 2 + (1 - co))

    sends = []

    def send(src, dst, sem, device):
        k = len(sends)
        copy = pltpu.make_async_remote_copy(
            src_ref=src, dst_ref=dst, send_sem=send_sem.at[k], recv_sem=sem,
            device_id=device, device_id_type=MESH,
        )
        copy.start()
        sends.append(copy)
        return copy

    locals_ = []

    def local(src, dst):
        copy = pltpu.make_async_copy(src, dst, local_sem.at[len(locals_)])
        copy.start()
        locals_.append(copy)
        return copy

    barrier = pltpu.get_barrier_semaphore()
    peers = [xh_peer, xl_peer, co_peer]
    for d in far_first(n):
        peers += [y_peer(d), z_peer(d)]
    for device in peers:
        pl.semaphore_signal(barrier, inc=1, device_id=device, device_id_type=MESH)
    own_ups = local(ups, ups_buf.at[q, y])
    own_gp = local(gate, gp_buf.at[row])
    own_up = local(upre, up_buf.at[row])
    own_wd = local(w_down, wd)
    own_tok = local(tok, tok_buf.at[q, y])
    own_wg = local(w_gate, wg)
    own_wu = local(w_up, wu)
    pl.semaphore_wait(barrier, len(peers))

    ups_y = {d: send(ups, ups_buf.at[q, y], ups_sem.at[d], y_peer(d)) for d in far_first(n)}
    gp_z, up_z = {}, {}
    for d in far_first(n):
        gp_z[d] = send(gate, gp_buf.at[row], gp_sem.at[d], z_peer(d))
        up_z[d] = send(upre, up_buf.at[row], up_sem.at[d], z_peer(d))
    tok_y = {d: send(tok, tok_buf.at[q, y], tok_sem.at[d], y_peer(d)) for d in far_first(n)}

    own_ups.wait()
    for d in near_first(n):
        ups_y[d].wait_recv()
    mine, theirs = ups_buf.at[q], ups_buf.at[(1 - xl) * 2 + co]
    ups_xl = send(mine, mine, quad_sem.at[0], xl_peer)
    ups_co = send(mine, mine, quad_sem.at[1], co_peer)
    ups_xl.wait_recv()
    ups_both = send(theirs, theirs, quad_sem.at[2], co_peer)
    own_wd.wait()
    ups_co.wait_recv()
    ups_both.wait_recv()

    def order_tokens(buf, out, first, count):
        @pl.loop(0, count)
        def _(k):
            rows = buf[:, first + k].astype(F32).reshape(32, buf.shape[-1])
            out[pl.ds(pl.multiple_of((first + k) * 32, 32), 32), :] = rows.astype(BF16)

    half = 16 * n
    near_rows = pl.ds(pl.multiple_of(xh * half, half), half)
    far_rows = pl.ds(pl.multiple_of(other * half, half), half)
    near_blocks, far_blocks = pl.ds(xh * n, n), pl.ds(other * n, n)

    order_tokens(ups_buf, ups_out, other * (n // 2), n // 2)
    part = lax.dot_general(ups_out[far_rows, :], wd[...], LAST, preferred_element_type=F32)
    x_send[...] = part.astype(BF16).reshape(x_send.shape)
    x_order = far_first(n) + [0]
    parts_x = {}
    for d in x_order:
        k = lax.rem(z + d, n)
        parts_x[d] = send(x_send.at[k], x_recv.at[k], xr_sem.at[d], xh_peer)
    order_tokens(ups_buf, ups_out, xh * (n // 2), n // 2)
    part = lax.dot_general(ups_out[near_rows, :], wd[...], LAST, preferred_element_type=F32)
    own_part[...] = part.reshape(own_part.shape)

    parts_z = {}
    for d in x_order:
        k = lax.rem(z + d, n)
        parts_x[d].wait_recv()
        total = own_part[k] + x_recv[k].astype(F32)
        if d:
            z_send[k] = total.astype(BF16)
            parts_z[d] = send(z_send.at[k], z_recv.at[d], zr_sem.at[d], z_peer(d))
        else:
            own_part[k] = total

    own_gp.wait()
    own_up.wait()
    for d in near_first(n):
        gp_z[d].wait_recv()
        up_z[d].wait_recv()
    gp_x = send(gp_buf.at[near_blocks], gp_buf.at[near_blocks], half_sem.at[0], xh_peer)
    up_x = send(up_buf.at[near_blocks], up_buf.at[near_blocks], half_sem.at[1], xh_peer)

    def activations(first):
        @pl.loop(0, n)
        def _(j):
            k = first + j
            g = gp_buf[k].astype(F32)
            u = up_buf[k].astype(F32)
            s = jax.nn.sigmoid(g)
            activated = g * s
            act[k] = activated
            slope_up[k] = u * (s * (1.0 + g * (1.0 - s)))
            hid_out[pl.ds(pl.multiple_of(k * 16, 16), 16), :] = (activated * u).astype(BF16)

    activations(xh * n)

    own_tok.wait()
    for d in near_first(n):
        tok_y[d].wait_recv()
    t_mine, t_theirs = tok_buf.at[q], tok_buf.at[(1 - xl) * 2 + co]
    tok_xl = send(t_mine, t_mine, quad_sem.at[3], xl_peer)
    tok_co = send(t_mine, t_mine, quad_sem.at[4], co_peer)

    total = own_part[z]
    for d in near_first(n):
        parts_z[d].wait_recv()
        total = total + z_recv[d].astype(F32)
    hg_buf[row] = total.astype(BF16)
    hg_mine = hg_buf.at[row]
    hg_z = {d: send(hg_mine, hg_mine, hz_sem.at[d], z_peer(d)) for d in far_first(n)}
    hg_x = [send(hg_mine, hg_mine, hx_sem.at[0], xh_peer)]

    gp_x.wait_recv()
    up_x.wait_recv()
    activations(other * n)
    tok_xl.wait_recv()
    tok_both = send(t_theirs, t_theirs, quad_sem.at[5], co_peer)
    own_wg.wait()
    own_wu.wait()

    for d in near_first(n):
        hg_z[d].wait_recv()
        block = hg_buf.at[xh * n + lax.rem(z - d + n, n)]
        hg_x.append(send(block, block, hx_sem.at[d], xh_peer))

    def deltas(first):
        @pl.loop(0, n)
        def _(j):
            k = first + j
            grad = hg_buf[k].astype(F32)
            rows = pl.ds(pl.multiple_of(k * 16, 16), 16)
            gd_out[rows, :] = (grad * slope_up[k]).astype(BF16)
            ud_out[rows, :] = (grad * act[k]).astype(BF16)

    def input_part(rows, blocks, sem):
        part = lax.dot_general(gd_out[rows, :], wg[...], LAST, preferred_element_type=F32)
        part = part + lax.dot_general(ud_out[rows, :], wu[...], LAST, preferred_element_type=F32)
        ig_part[blocks] = part.reshape(n, 2, 8, part.shape[-1])
        return send(ig_part.at[blocks, 1 - co], core_recv.at[blocks], sem, co_peer)

    def to_xl(first, sem):
        @pl.loop(0, n // 2)
        def _(j):
            k = 2 * (first + j) + 1 - xl
            xl_send[first + j] = (ig_part[k, co] + core_recv[k]).astype(BF16)

        blocks = pl.ds(first, n // 2)
        return send(xl_send.at[blocks], xl_recv.at[blocks], sem, xl_peer)

    deltas(xh * n)
    near_co = input_part(near_rows, near_blocks, ig_sem.at[0])
    for copy in hg_x:
        copy.wait_recv()
    deltas(other * n)
    near_co.wait_recv()
    near_xl = to_xl(xh * (n // 2), ig_sem.at[2])
    far_co = input_part(far_rows, far_blocks, ig_sem.at[1])
    far_co.wait_recv()
    far_xl = to_xl(other * (n // 2), ig_sem.at[3])

    def ig_block(k):
        return ig_part[2 * k + xl, co] + core_recv[2 * k + xl] + xl_recv[k].astype(F32)

    near_xl.wait_recv()
    far_xl.wait_recv()
    ig_y = {}
    for d in far_first(n):
        k = lax.rem(y + d, n)
        y_send[k] = ig_block(k).astype(BF16)
        ig_y[d] = send(y_send.at[k], y_recv.at[d], ig_y_sem.at[d], y_peer(d))
    total = ig_block(y)

    tok_co.wait_recv()
    tok_both.wait_recv()
    order_tokens(tok_buf, tok_out, 0, n)

    for d in near_first(n):
        ig_y[d].wait_recv()
        total = total + y_recv[d].astype(F32)
    ig_out[...] = total.astype(BF16)

    for copy in sends:
        copy.wait_send()


def weight_grads(scale, ig, gd, ud, hid, tok, ups, input_grad, gate_grad, up_grad, down_grad):
    def scaled(a, b):
        return (lax.dot_general(a, b, FIRST, preferred_element_type=F32) * scale).astype(BF16)

    input_grad[...] = ig[...]
    gate_grad[...] = scaled(tok[...], gd[...])
    up_grad[...] = scaled(tok[...], ud[...])
    down_grad[...] = scaled(hid[...], ups[...])


def on_device(n, tokens, upstream, gate_pre, up_pre, w_gate, w_up, w_down):
    d_block, f_block = w_gate.shape
    total = 32 * n
    blocks = 2 * n
    dma = pltpu.SemaphoreType.DMA
    hbm_spec = pl.BlockSpec(memory_space=pltpu.HBM)
    vmem_spec = pl.BlockSpec(memory_space=pltpu.VMEM)
    n_sends = 7 * (n - 1) + n + 1 + 2 + 6 + 4 + (n - 1) + 1
    ig, gd, ud, hid, tok, ups = pl.pallas_call(
        functools.partial(exchange, n),
        name="exchange",
        out_shape=(
            jax.ShapeDtypeStruct((8, d_block), BF16),
            jax.ShapeDtypeStruct((total, f_block), BF16),
            jax.ShapeDtypeStruct((total, f_block), BF16),
            jax.ShapeDtypeStruct((total, f_block), BF16),
            jax.ShapeDtypeStruct((total, d_block), BF16),
            jax.ShapeDtypeStruct((total, d_block), BF16),
        ),
        in_specs=[hbm_spec] * 7,
        out_specs=[vmem_spec] * 6,
        scratch_shapes=[
            pltpu.VMEM((d_block, f_block), BF16),
            pltpu.VMEM((d_block, f_block), BF16),
            pltpu.VMEM((f_block, d_block), BF16),
            pltpu.VMEM((4, n, 8, d_block), BF16),
            pltpu.VMEM((4, n, 8, d_block), BF16),
            pltpu.VMEM((blocks, 16, f_block), BF16),
            pltpu.VMEM((blocks, 16, f_block), BF16),
            pltpu.VMEM((n, 16, f_block), F32),
            pltpu.VMEM((n, 16, f_block), BF16),
            pltpu.VMEM((n, 16, f_block), BF16),
            pltpu.VMEM((n, 16, f_block), BF16),
            pltpu.VMEM((n, 16, f_block), BF16),
            pltpu.VMEM((blocks, 16, f_block), BF16),
            pltpu.VMEM((blocks, 16, f_block), F32),
            pltpu.VMEM((blocks, 16, f_block), F32),
            pltpu.VMEM((blocks, 2, 8, d_block), F32),
            pltpu.VMEM((blocks, 8, d_block), F32),
            pltpu.VMEM((n, 8, d_block), BF16),
            pltpu.VMEM((n, 8, d_block), BF16),
            pltpu.VMEM((n, 8, d_block), BF16),
            pltpu.VMEM((n, 8, d_block), BF16),
            dma((7,)),
            dma((n_sends,)),
            dma((n,)), dma((n,)), dma((n,)), dma((n,)),
            dma((2,)), dma((6,)),
            dma((n,)), dma((n,)), dma((n,)), dma((n,)),
            dma((4,)), dma((n,)),
        ],
        compiler_params=pltpu.CompilerParams(
            collective_id=0, has_side_effects=True, vmem_limit_bytes=40 * 1024 * 1024
        ),
    )(*(
        pltpu.with_memory_space_constraint(a, pltpu.HBM)
        for a in (upstream, tokens, gate_pre, up_pre, w_gate, w_up, w_down)
    ))

    scale = float(total) ** -0.5
    input_grad, gate_grad, up_grad, down_grad = pl.pallas_call(
        functools.partial(weight_grads, scale),
        name="weight_grads",
        grid=(2,),
        in_specs=[
            pl.BlockSpec((8, d_block), lambda i: (0, 0)),
            pl.BlockSpec((total, f_block), lambda i: (0, 0)),
            pl.BlockSpec((total, f_block), lambda i: (0, 0)),
            pl.BlockSpec((total, f_block // 2), lambda i: (0, i)),
            pl.BlockSpec((total, d_block // 2), lambda i: (0, i)),
            pl.BlockSpec((total, d_block), lambda i: (0, 0)),
        ],
        out_specs=[
            pl.BlockSpec((8, d_block), lambda i: (0, 0)),
            pl.BlockSpec((d_block // 2, f_block), lambda i: (i, 0)),
            pl.BlockSpec((d_block // 2, f_block), lambda i: (i, 0)),
            pl.BlockSpec((f_block // 2, d_block), lambda i: (i, 0)),
        ],
        out_shape=(
            jax.ShapeDtypeStruct((8, d_block), BF16),
            jax.ShapeDtypeStruct((d_block, f_block), BF16),
            jax.ShapeDtypeStruct((d_block, f_block), BF16),
            jax.ShapeDtypeStruct((f_block, d_block), BF16),
        ),
        compiler_params=pltpu.CompilerParams(vmem_limit_bytes=24 * 1024 * 1024),
    )(ig, gd, ud, hid, tok, ups)
    return (input_grad, gate_grad, up_grad, down_grad)


def solution(mesh):
    placed = (
        P("col", "row"),
        P("col", "row"),
        P("row", "col"),
        P("row", "col"),
        P("row", "col"),
        P("row", "col"),
        P("col", "row"),
    )
    return jax.shard_map(
        functools.partial(on_device, mesh.shape["row"] // 2),
        mesh=mesh,
        in_specs=placed,
        out_specs=(P("col", "row"), P("row", "col"), P("row", "col"), P("col", "row")),
        check_vma=False,
    )
```

time: 459 us -> 59.9 us (0.13)
  the two profiles are of different devices: /device:TPU:7 before, /device:TPU:1 now
where the time goes in v1:
time: 59.9 us; the launch traced here: 59.8 us
  Pallas kernels  59.2 us (99%)
  between operations  0.64 us (1%)
    pallas_call x1, Pallas kernels, on_device(): pl.pallas_call(functools.partial(exchange, n), name='exchange', out_shape...  57.2 us
    pallas_call x1, Pallas kernels, on_device(): pl.pallas_call(functools.partial(weight_grads, scale), name='weight_grads...  1.96 us

profile of v1, /device:TPU:1, one launch (start us, length us, event | category | flops | bytes accessed | tf_op | source)
XLA Modules:
  0.0 59.8 jit_solution(2598847669604347581)
XLA Ops:
  0.6 57.2 %exchange.1 = (bf16[8,512]{1,0:T(8,128)(2,1)S(1)}, bf16[256,768]{1,0:T(8,128)(2,1)S(1)}, bf16[256,768]{1,0:T(8,128)(2,1)S(1)}, bf16[256,768]{1,0:T(8,128)(2,1)S(...) custom-call(bf16[8,512]{1,0:T(8,128)(2,1)} %ups.1, bf16[8,512]{1,0:T(8,128)(2,1)} %tok.1, ...), custom_call_target="tpu_custom_call" | custom-call | tf_op jit(solution)/shard_map/exchange/pallas_call | solution.py:267
  57.8 2.0 %weight_grads.1 = (bf16[8,512]{1,0:T(8,128)(2,1)}, bf16[512,768]{1,0:T(8,128)(2,1)}, bf16[512,768]{1,0:T(8,128)(2,1)}, bf16[768,512]{1,0:T(8,128)(2,1)}) custom-call(bf16[8,512]{1,0:T(8,128)(2,1)S(1)} %get-tuple-element.10.ig, bf16[256,768]{1,0:T(8,128)(2,1)S(1)} %get-tuple-element.11.gd, bf16[256,768]{1,0:T(8,128)(2,1)S(1)} %get-tuple-element.12.ud, ...), custom_call_target="tpu_custom_call" | custom-call | tf_op jit(solution)/shard_map/weight_grads/pallas_call | solution.py:318

commit v2 on v1

v2 whole, which is shorter than its diff:
```python
import functools

import jax
import jax.numpy as jnp
from jax import lax
from jax.experimental import pallas as pl
from jax.experimental.pallas import tpu as pltpu
from jax.sharding import PartitionSpec as P

MESH = pl.DeviceIdType.MESH
F32 = jnp.float32
BF16 = jnp.bfloat16
LAST = (((1,), (1,)), ((), ()))
FIRST = (((0,), (0,)), ((), ()))


def far_first(n):
    return sorted(range(1, n), key=lambda d: (-min(d, n - d), d))


def near_first(n):
    return sorted(range(1, n), key=lambda d: (min(d, n - d), d))


def exchange(
    n,
    ups, tok, gate, upre, w_gate, w_up, w_down,
    ig_out, gd_out, ud_out, hid_out, tok_out, ups_out,
    wg, wu, wd, ups_buf, tok_buf, gu_buf, part_buf, x_send, x_recv, z_send, z_recv,
    hg_buf, act, slope_up, ig_part, core_recv, y_send, y_recv,
    local_sem, send_sem, tok_sem, gu_sem, pair_sem,
    xr_sem, zr_sem, hz_sem, hx_sem, ig_y_sem, late_sem, ups_sem,
):
    row, col = lax.axis_index("row"), lax.axis_index("col")
    xh, z = row // n, lax.rem(row, n)
    y, q = col // 4, lax.rem(col, 4)
    xl, co = q // 2, lax.rem(q, 2)
    other = 1 - xh

    def z_peer(d):
        return (xh * n + lax.rem(z + d, n), col)

    def y_peer(d):
        return (row, lax.rem(y + d, n) * 4 + q)

    def yx_peer(d, e):
        return (row, lax.rem(y + d, n) * 4 + lax.rem(xl + e, 2) * 2 + co)

    offsets = [(d, e) for d in range(n) for e in range(2) if d or e]
    offsets.sort(key=lambda t: -min(t[0], n - t[0]) - t[1])
    xh_peer = (other * n + z, col)
    xl_peer = (row, y * 4 + (1 - xl) * 2 + co)
    co_peer = (row, y * 4 + xl * 2 + (1 - co))

    sends = []

    def send(src, dst, sem, device):
        copy = pltpu.make_async_remote_copy(
            src_ref=src, dst_ref=dst, send_sem=send_sem.at[len(sends)], recv_sem=sem,
            device_id=device, device_id_type=MESH,
        )
        copy.start()
        sends.append(copy)
        return copy

    def share(block, sem, device):
        return send(block, block, sem, device)

    locals_ = []

    def local(src, dst):
        copy = pltpu.make_async_copy(src, dst, local_sem.at[len(locals_)])
        copy.start()
        locals_.append(copy)
        return copy

    def wait_all(copies):
        for copy in copies:
            copy.wait_recv()

    barrier = pltpu.get_barrier_semaphore()
    peers = [yx_peer(d, e) for d, e in offsets] + [z_peer(d) for d in far_first(n)]
    peers += [xh_peer, co_peer]
    for device in peers:
        pl.semaphore_signal(barrier, inc=1, device_id=device, device_id_type=MESH)
    first_copies = [
        local(ups, ups_buf.at[co, y, xl]),
        local(gate, gu_buf.at[row, 0]),
        local(upre, gu_buf.at[row, 1]),
        local(tok, tok_buf.at[co, y, xl]),
    ]
    for copy in first_copies:
        copy.wait()
    pl.semaphore_wait(barrier, len(peers))

    ups_y = [share(ups_buf.at[co, y, xl], ups_sem.at[d, e], yx_peer(d, e)) for d, e in offsets]
    own_wd = local(w_down, wd)
    gu_z = [share(gu_buf.at[row], gu_sem.at[d], z_peer(d)) for d in near_first(n)]
    tok_xl = share(tok_buf.at[co, y, xl], pair_sem.at[1], xl_peer)
    wait_all(ups_y[::-1])
    ups_co = share(ups_buf.at[co], pair_sem.at[2], co_peer)
    tok_xl.wait_recv()
    tok_y = [share(tok_buf.at[co, y], tok_sem.at[d], y_peer(d)) for d in far_first(n)]

    half = 16 * n
    near_rows = pl.ds(pl.multiple_of(xh * half, half), half)
    far_rows = pl.ds(pl.multiple_of(other * half, half), half)
    near_blocks, far_blocks = pl.ds(xh * n, n), pl.ds(other * n, n)

    def hidden_part(core):
        rows = ups_buf[core].astype(F32).reshape(half, ups.shape[-1]).astype(BF16)
        part = lax.dot_general(rows, wd[...], LAST, preferred_element_type=F32)
        part_buf[core] = part.reshape(2 * n, 8, part.shape[-1])

    own_wd.wait()
    hidden_part(co)

    x_send[co] = part_buf[co, far_blocks].astype(BF16)
    first_x = send(x_send.at[co], x_recv.at[co], xr_sem.at[n], xh_peer)
    ups_co.wait_recv()
    hidden_part(1 - co)
    x_order = far_first(n) + [0]
    parts_x = []
    for d in x_order:
        k = lax.rem(z + d, n)
        x_send[1 - co, k] = part_buf[1 - co, other * n + k].astype(BF16)
        parts_x.append(send(x_send.at[1 - co, k], x_recv.at[1 - co, k], xr_sem.at[d], xh_peer))
    own_wg = local(w_gate, wg)
    own_wu = local(w_up, wu)

    def order_tokens(buf, out):
        @pl.loop(0, n)
        def _(k):
            rows = jnp.stack([buf[0, k].astype(F32), buf[1, k].astype(F32)], axis=1)
            rows = rows.reshape(32, buf.shape[-1])
            out[pl.ds(pl.multiple_of(k * 32, 32), 32), :] = rows.astype(BF16)

    order_tokens(ups_buf, ups_out)

    parts_z = []
    first_x.wait_recv()
    for d, part_x in zip(x_order, parts_x):
        k = lax.rem(z + d, n)
        part_x.wait_recv()
        total = part_buf[:, xh * n + k] + x_recv[:, k].astype(F32)
        if d:
            z_send[k] = total.astype(BF16)
            parts_z.append(send(z_send.at[k], z_recv.at[d], zr_sem.at[d], z_peer(d)))
    part_buf[:, row] = total

    wait_all(gu_z)
    gu_x = share(gu_buf.at[near_blocks], gu_sem.at[0], xh_peer)
    wait_all(tok_y)
    tok_co = share(tok_buf.at[co], pair_sem.at[3], co_peer)

    def activations(first):
        @pl.loop(0, n)
        def _(j):
            k = first + j
            g = gu_buf[k, 0].astype(F32)
            u = gu_buf[k, 1].astype(F32)
            s = jax.nn.sigmoid(g)
            activated = g * s
            act[k] = activated
            slope_up[k] = u * (s * (1.0 + g * (1.0 - s)))
            hid_out[pl.ds(pl.multiple_of(k * 16, 16), 16), :] = (activated * u).astype(BF16)

    activations(xh * n)

    total = part_buf[:, row]
    for d, part_z in zip(far_first(n)[::-1], parts_z[::-1]):
        part_z.wait_recv()
        total = total + z_recv[d].astype(F32)
    hg_buf[row] = total.reshape(16, total.shape[-1]).astype(BF16)
    hg_z = [share(hg_buf.at[row], hz_sem.at[d], z_peer(d)) for d in near_first(n)]
    hg_x = [share(hg_buf.at[row], hx_sem.at[0], xh_peer)]

    tok_co.wait_recv()
    order_tokens(tok_buf, tok_out)
    own_wg.wait()
    own_wu.wait()

    for d, copy in zip(near_first(n), hg_z):
        copy.wait_recv()
        block = hg_buf.at[xh * n + lax.rem(z - d + n, n)]
        hg_x.append(share(block, hx_sem.at[d], xh_peer))

    def deltas(first):
        @pl.loop(0, n)
        def _(j):
            k = first + j
            grad = hg_buf[k].astype(F32)
            rows = pl.ds(pl.multiple_of(k * 16, 16), 16)
            gd_out[rows, :] = (grad * slope_up[k]).astype(BF16)
            ud_out[rows, :] = (grad * act[k]).astype(BF16)

    def input_part(rows, blocks, sem):
        part = lax.dot_general(gd_out[rows, :], wg[...], LAST, preferred_element_type=F32)
        part = part + lax.dot_general(ud_out[rows, :], wu[...], LAST, preferred_element_type=F32)
        ig_part[blocks] = part.reshape(n, 2, 8, part.shape[-1])
        return send(ig_part.at[blocks, 1 - co], core_recv.at[blocks], sem, co_peer)

    def pair_sum(k):
        return ig_part[k, co] + core_recv[k]

    late = []

    def to_y(first):
        for j in range(n):
            k = first + j
            y_send[k] = pair_sum(k).astype(BF16)
            copy = pltpu.make_async_remote_copy(
                src_ref=y_send.at[k], dst_ref=y_recv.at[2 * y + xl],
                send_sem=late_sem.at[len(late)], recv_sem=ig_y_sem.at[2 * y + xl],
                device_id=(row, k * 2 + co), device_id_type=MESH,
            )
            late.append((k, copy))

            @pl.when(k != 2 * y + xl)
            def _():
                copy.start()

    deltas(xh * n)
    near_co = input_part(near_rows, near_blocks, pair_sem.at[4])
    gu_x.wait_recv()
    activations(other * n)
    wait_all(hg_x)
    deltas(other * n)
    far_co = input_part(far_rows, far_blocks, pair_sem.at[5])
    near_co.wait_recv()
    to_y(xh * n)
    far_co.wait_recv()
    to_y(other * n)

    total = pair_sum(2 * y + xl)
    for d, e in offsets[::-1]:
        k = 2 * lax.rem(y - d + n, n) + lax.rem(xl + e, 2)
        pltpu.make_async_remote_copy(
            src_ref=y_send.at[k], dst_ref=y_recv.at[k], send_sem=send_sem.at[0],
            recv_sem=ig_y_sem.at[k], device_id=co_peer, device_id_type=MESH,
        ).wait_recv()
        total = total + y_recv[k].astype(F32)
    ig_out[...] = total.astype(BF16)

    for copy in sends:
        copy.wait_send()
    for k, copy in late:

        @pl.when(k != 2 * y + xl)
        def _():
            copy.wait_send()


def weight_grads(
    scale, ig, gd, ud, hid, tok, ups, input_grad, gate_grad, up_grad, down_grad,
    gate_buf, up_buf, down_buf, sem,
):
    copies = []

    def chunk(a, first, rows, b, buf, out):
        left = a[:, first : first + rows]
        part = lax.dot_general(left, b[...], FIRST, preferred_element_type=F32) * scale
        buf[pl.ds(first, rows), :] = part.astype(BF16)
        copies.append(
            pltpu.make_async_copy(
                buf.at[pl.ds(first, rows)], out.at[pl.ds(first, rows)], sem.at[len(copies)]
            )
        )
        copies[-1].start()

    copies.append(pltpu.make_async_copy(ig, input_grad, sem.at[0]))
    copies[-1].start()
    for a, b, buf, out in (
        (tok, gd, gate_buf, gate_grad), (tok, ud, up_buf, up_grad), (hid, ups, down_buf, down_grad)
    ):
        for first in range(0, a.shape[1], 256):
            chunk(a, first, 256, b, buf, out)
    for copy in copies:
        copy.wait()


def on_device(n, tokens, upstream, gate_pre, up_pre, w_gate, w_up, w_down):
    d_block, f_block = w_gate.shape
    total = 32 * n
    blocks = 2 * n
    dma = pltpu.SemaphoreType.DMA
    hbm_spec = pl.BlockSpec(memory_space=pltpu.HBM)
    vmem_spec = pl.BlockSpec(memory_space=pltpu.VMEM)
    n_sends = 8 * n + 2
    ig, gd, ud, hid, tok, ups = pl.pallas_call(
        functools.partial(exchange, n),
        name="exchange",
        out_shape=(
            jax.ShapeDtypeStruct((8, d_block), BF16),
            jax.ShapeDtypeStruct((total, f_block), BF16),
            jax.ShapeDtypeStruct((total, f_block), BF16),
            jax.ShapeDtypeStruct((total, f_block), BF16),
            jax.ShapeDtypeStruct((total, d_block), BF16),
            jax.ShapeDtypeStruct((total, d_block), BF16),
        ),
        in_specs=[hbm_spec] * 7,
        out_specs=[vmem_spec] * 6,
        scratch_shapes=[
            pltpu.VMEM((d_block, f_block), BF16),
            pltpu.VMEM((d_block, f_block), BF16),
            pltpu.VMEM((f_block, d_block), BF16),
            pltpu.VMEM((2, n, 2, 8, d_block), BF16),
            pltpu.VMEM((2, n, 2, 8, d_block), BF16),
            pltpu.VMEM((blocks, 2, 16, f_block), BF16),
            pltpu.VMEM((2, blocks, 8, f_block), F32),
            pltpu.VMEM((2, n, 8, f_block), BF16),
            pltpu.VMEM((2, n, 8, f_block), BF16),
            pltpu.VMEM((n, 2, 8, f_block), BF16),
            pltpu.VMEM((n, 2, 8, f_block), BF16),
            pltpu.VMEM((blocks, 16, f_block), BF16),
            pltpu.VMEM((blocks, 16, f_block), F32),
            pltpu.VMEM((blocks, 16, f_block), F32),
            pltpu.VMEM((blocks, 2, 8, d_block), F32),
            pltpu.VMEM((blocks, 8, d_block), F32),
            pltpu.VMEM((blocks, 8, d_block), BF16),
            pltpu.VMEM((blocks, 8, d_block), BF16),
            dma((7,)),
            dma((n_sends,)),
            dma((n,)), dma((n,)), dma((7,)),
            dma((n + 1,)), dma((n,)), dma((n,)), dma((n,)), dma((2 * n,)), dma((2 * n,)), dma((n, 2)),
        ],
        compiler_params=pltpu.CompilerParams(
            collective_id=0, has_side_effects=True, vmem_limit_bytes=40 * 1024 * 1024
        ),
    )(*(
        pltpu.with_memory_space_constraint(a, pltpu.HBM)
        for a in (upstream, tokens, gate_pre, up_pre, w_gate, w_up, w_down)
    ))

    scale = float(total) ** -0.5
    input_grad, gate_grad, up_grad, down_grad = pl.pallas_call(
        functools.partial(weight_grads, scale),
        name="weight_grads",
        in_specs=[vmem_spec] * 6,
        out_specs=[pl.BlockSpec(memory_space=pl.ANY)] * 4,
        out_shape=(
            jax.ShapeDtypeStruct((8, d_block), BF16),
            jax.ShapeDtypeStruct((d_block, f_block), BF16),
            jax.ShapeDtypeStruct((d_block, f_block), BF16),
            jax.ShapeDtypeStruct((f_block, d_block), BF16),
        ),
        scratch_shapes=[
            pltpu.VMEM((d_block, f_block), BF16),
            pltpu.VMEM((d_block, f_block), BF16),
            pltpu.VMEM((f_block, d_block), BF16),
            dma((1 + (2 * d_block + f_block) // 256,)),
        ],
        compiler_params=pltpu.CompilerParams(vmem_limit_bytes=24 * 1024 * 1024),
    )(ig, gd, ud, hid, tok, ups)
    return (input_grad, gate_grad, up_grad, down_grad)


def solution(mesh):
    placed = (
        P("col", "row"),
        P("col", "row"),
        P("row", "col"),
        P("row", "col"),
        P("row", "col"),
        P("row", "col"),
        P("col", "row"),
    )
    return jax.shard_map(
        functools.partial(on_device, mesh.shape["row"] // 2),
        mesh=mesh,
        in_specs=placed,
        out_specs=(P("col", "row"), P("row", "col"), P("row", "col"), P("col", "row")),
        check_vma=False,
    )
```

time: 59.9 us -> 52.1 us (0.87)
  the two profiles are of different devices: /device:TPU:1 before, /device:TPU:7 now
where the time goes in v2:
time: 52.1 us; the launch traced here: 51.9 us
  Pallas kernels  51.3 us (98%)
  between operations  0.64 us (1%)
    pallas_call x1, Pallas kernels, on_device(): pl.pallas_call(functools.partial(exchange, n), name='exchange', out_shape...  49.5 us
    pallas_call x1, Pallas kernels, on_device(): pl.pallas_call(functools.partial(weight_grads, scale), name='weight_grads...  1.79 us

profile of v2, /device:TPU:7, one launch (start us, length us, event | category | flops | bytes accessed | tf_op | source)
XLA Modules:
  0.0 51.9 jit_solution(4393982034589080651)
XLA Ops:
  0.6 49.5 %exchange.1 = (bf16[8,512]{1,0:T(8,128)(2,1)S(1)}, bf16[256,768]{1,0:T(8,128)(2,1)S(1)}, bf16[256,768]{1,0:T(8,128)(2,1)S(1)}, bf16[256,768]{1,0:T(8,128)(2,1)S(...) custom-call(bf16[8,512]{1,0:T(8,128)(2,1)} %ups.1, bf16[8,512]{1,0:T(8,128)(2,1)} %tok.1, ...), custom_call_target="tpu_custom_call" | custom-call | tf_op jit(solution)/shard_map/exchange/pallas_call | solution.py:290
  50.1 1.8 %weight_grads.1 = (bf16[8,512]{1,0:T(8,128)(2,1)}, bf16[512,768]{1,0:T(8,128)(2,1)}, bf16[512,768]{1,0:T(8,128)(2,1)}, bf16[768,512]{1,0:T(8,128)(2,1)}) custom-call(bf16[8,512]{1,0:T(8,128)(2,1)S(1)} %get-tuple-element.10.ig, bf16[256,768]{1,0:T(8,128)(2,1)S(1)} %get-tuple-element.11.gd, bf16[256,768]{1,0:T(8,128)(2,1)S(1)} %get-tuple-element.12.ud, ...), custom_call_target="tpu_custom_call" | custom-call | tf_op jit(solution)/shard_map/weight_grads/pallas_call | solution.py:336

commit v3 on v2

--- a/solution.py
+++ b/solution.py
@@ -23,9 +23,10 @@
 
 
 def exchange(
-    n,
+    n, scale,
     ups, tok, gate, upre, w_gate, w_up, w_down,
-    ig_out, gd_out, ud_out, hid_out, tok_out, ups_out,
+    ig_out, gate_out, up_out, down_out,
+    gd_out, ud_out, hid_out, tok_out, ups_out,
     wg, wu, wd, ups_buf, tok_buf, gu_buf, part_buf, x_send, x_recv, z_send, z_recv,
     hg_buf, act, slope_up, ig_part, core_recv, y_send, y_recv,
     local_sem, send_sem, tok_sem, gu_sem, pair_sem,
@@ -81,20 +82,21 @@
     barrier = pltpu.get_barrier_semaphore()
     peers = [yx_peer(d, e) for d, e in offsets] + [z_peer(d) for d in far_first(n)]
     peers += [xh_peer, co_peer]
+    first_copies = [local(ups, ups_buf.at[co, y, xl])]
     for device in peers:
         pl.semaphore_signal(barrier, inc=1, device_id=device, device_id_type=MESH)
-    first_copies = [
-        local(ups, ups_buf.at[co, y, xl]),
+    first_copies += [
         local(gate, gu_buf.at[row, 0]),
         local(upre, gu_buf.at[row, 1]),
         local(tok, tok_buf.at[co, y, xl]),
     ]
-    for copy in first_copies:
-        copy.wait()
+    first_copies[0].wait()
     pl.semaphore_wait(barrier, len(peers))
 
     ups_y = [share(ups_buf.at[co, y, xl], ups_sem.at[d, e], yx_peer(d, e)) for d, e in offsets]
     own_wd = local(w_down, wd)
+    for copy in first_copies[1:]:
+        copy.wait()
     gu_z = [share(gu_buf.at[row], gu_sem.at[d], z_peer(d)) for d in near_first(n)]
     tok_xl = share(tok_buf.at[co, y, xl], pair_sem.at[1], xl_peer)
     wait_all(ups_y[::-1])
@@ -172,8 +174,8 @@
         part_z.wait_recv()
         total = total + z_recv[d].astype(F32)
     hg_buf[row] = total.reshape(16, total.shape[-1]).astype(BF16)
+    hg_x = [share(hg_buf.at[row], hx_sem.at[0], xh_peer)]
     hg_z = [share(hg_buf.at[row], hz_sem.at[d], z_peer(d)) for d in near_first(n)]
-    hg_x = [share(hg_buf.at[row], hx_sem.at[0], xh_peer)]
 
     tok_co.wait_recv()
     order_tokens(tok_buf, tok_out)
@@ -232,6 +234,19 @@
     far_co.wait_recv()
     to_y(other * n)
 
+    @pl.loop(0, tok_out.shape[1] // 256)
+    def _(i):
+        columns = pl.ds(pl.multiple_of(i * 256, 256), 256)
+        for delta, out in ((gd_out, gate_out), (ud_out, up_out)):
+            part = lax.dot_general(tok_out[:, columns], delta[...], FIRST, preferred_element_type=F32)
+            out[columns, :] = (part * scale).astype(BF16)
+
+    @pl.loop(0, hid_out.shape[1] // 256)
+    def _(i):
+        columns = pl.ds(pl.multiple_of(i * 256, 256), 256)
+        part = lax.dot_general(hid_out[:, columns], ups_out[...], FIRST, preferred_element_type=F32)
+        down_out[columns, :] = (part * scale).astype(BF16)
+
     total = pair_sum(2 * y + xl)
     for d, e in offsets[::-1]:
         k = 2 * lax.rem(y - d + n, n) + lax.rem(xl + e, 2)
@@ -251,30 +266,19 @@
             copy.wait_send()
 
 
-def weight_grads(
-    scale, ig, gd, ud, hid, tok, ups, input_grad, gate_grad, up_grad, down_grad,
-    gate_buf, up_buf, down_buf, sem,
-):
+def write_out(*refs):
+    *pairs, sem = refs
     copies = []
-
-    def chunk(a, first, rows, b, buf, out):
-        left = a[:, first : first + rows]
-        part = lax.dot_general(left, b[...], FIRST, preferred_element_type=F32) * scale
-        buf[pl.ds(first, rows), :] = part.astype(BF16)
-        copies.append(
-            pltpu.make_async_copy(
-                buf.at[pl.ds(first, rows)], out.at[pl.ds(first, rows)], sem.at[len(copies)]
+    for src, dst in zip(pairs[:4], pairs[4:]):
+        parts = 1 if src.shape[0] < 256 else 2
+        rows = src.shape[0] // parts
+        for k in range(parts):
+            copies.append(
+                pltpu.make_async_copy(
+                    src.at[pl.ds(k * rows, rows)], dst.at[pl.ds(k * rows, rows)], sem.at[len(copies)]
+                )
             )
-        )
-        copies[-1].start()
-
-    copies.append(pltpu.make_async_copy(ig, input_grad, sem.at[0]))
-    copies[-1].start()
-    for a, b, buf, out in (
-        (tok, gd, gate_buf, gate_grad), (tok, ud, up_buf, up_grad), (hid, ups, down_buf, down_grad)
-    ):
-        for first in range(0, a.shape[1], 256):
-            chunk(a, first, 256, b, buf, out)
+            copies[-1].start()
     for copy in copies:
         copy.wait()
 
@@ -287,20 +291,24 @@
     hbm_spec = pl.BlockSpec(memory_space=pltpu.HBM)
     vmem_spec = pl.BlockSpec(memory_space=pltpu.VMEM)
     n_sends = 8 * n + 2
-    ig, gd, ud, hid, tok, ups = pl.pallas_call(
-        functools.partial(exchange, n),
+    grad_shapes = (
+        jax.ShapeDtypeStruct((8, d_block), BF16),
+        jax.ShapeDtypeStruct((d_block, f_block), BF16),
+        jax.ShapeDtypeStruct((d_block, f_block), BF16),
+        jax.ShapeDtypeStruct((f_block, d_block), BF16),
+    )
+    grads = pl.pallas_call(
+        functools.partial(exchange, n, float(total) ** -0.5),
         name="exchange",
-        out_shape=(
-            jax.ShapeDtypeStruct((8, d_block), BF16),
-            jax.ShapeDtypeStruct((total, f_block), BF16),
-            jax.ShapeDtypeStruct((total, f_block), BF16),
-            jax.ShapeDtypeStruct((total, f_block), BF16),
-            jax.ShapeDtypeStruct((total, d_block), BF16),
-            jax.ShapeDtypeStruct((total, d_block), BF16),
-        ),
+        out_shape=grad_shapes,
         in_specs=[hbm_spec] * 7,
-        out_specs=[vmem_spec] * 6,
+        out_specs=[vmem_spec] * 4,
         scratch_shapes=[
+            pltpu.VMEM((total, f_block), BF16),
+            pltpu.VMEM((total, f_block), BF16),
+            pltpu.VMEM((total, f_block), BF16),
+            pltpu.VMEM((total, d_block), BF16),
+            pltpu.VMEM((total, d_block), BF16),
             pltpu.VMEM((d_block, f_block), BF16),
             pltpu.VMEM((d_block, f_block), BF16),
             pltpu.VMEM((f_block, d_block), BF16),
@@ -332,27 +340,15 @@
         for a in (upstream, tokens, gate_pre, up_pre, w_gate, w_up, w_down)
     ))
 
-    scale = float(total) ** -0.5
-    input_grad, gate_grad, up_grad, down_grad = pl.pallas_call(
-        functools.partial(weight_grads, scale),
-        name="weight_grads",
-        in_specs=[vmem_spec] * 6,
+    return pl.pallas_call(
+        write_out,
+        name="write_out",
+        in_specs=[vmem_spec] * 4,
         out_specs=[pl.BlockSpec(memory_space=pl.ANY)] * 4,
-        out_shape=(
-            jax.ShapeDtypeStruct((8, d_block), BF16),
-            jax.ShapeDtypeStruct((d_block, f_block), BF16),
-            jax.ShapeDtypeStruct((d_block, f_block), BF16),
-            jax.ShapeDtypeStruct((f_block, d_block), BF16),
-        ),
-        scratch_shapes=[
-            pltpu.VMEM((d_block, f_block), BF16),
-            pltpu.VMEM((d_block, f_block), BF16),
-            pltpu.VMEM((f_block, d_block), BF16),
-            dma((1 + (2 * d_block + f_block) // 256,)),
-        ],
-        compiler_params=pltpu.CompilerParams(vmem_limit_bytes=24 * 1024 * 1024),
-    )(ig, gd, ud, hid, tok, ups)
-    return (input_grad, gate_grad, up_grad, down_grad)
+        out_shape=grad_shapes,
+        scratch_shapes=[dma((7,))],
+        compiler_params=pltpu.CompilerParams(vmem_limit_bytes=16 * 1024 * 1024),
+    )(*grads)
 
 
 def solution(mesh):

time: 52.1 us -> 51.6 us (level)
  Pallas kernels: 51.3 us -> 50.7 us
where the time goes in v3:
time: 51.6 us; the launch traced here: 51.4 us
  Pallas kernels  50.7 us (98%)
  between operations  0.64 us (1%)
    pallas_call x1, Pallas kernels, on_device(): pl.pallas_call(functools.partial(exchange, n, float(total) ** (-0.5)), na...  49.3 us
    pallas_call x1, Pallas kernels, on_device(): pl.pallas_call(write_out, name='write_out', in_specs=[vmem_spec] * 4, out...  1.46 us

profile of v3, /device:TPU:7, one launch (start us, length us, event | category | flops | bytes accessed | tf_op | source)
XLA Modules:
  0.0 51.4 jit_solution(4225973386464639264)
XLA Ops:
  0.6 49.3 %exchange.1 = (bf16[8,512]{1,0:T(8,128)(2,1)S(1)}, bf16[512,768]{1,0:T(8,128)(2,1)S(1)}, bf16[512,768]{1,0:T(8,128)(2,1)S(1)}, bf16[768,512]{1,0:T(8,128)(2,1)S(1)}) custom-call(bf16[8,512]{1,0:T(8,128)(2,1)} %ups.1, bf16[8,512]{1,0:T(8,128)(2,1)} %tok.1, bf16[16,768]{1,0:T(8,128)(2,1)} %gate.1, bf16[16,768]{1,0:T(8,128)(2,1)} %upre.1, ...), custom_call_target="tpu_custom_call" | custom-call | tf_op jit(solution)/shard_map/exchange/pallas_call | solution.py:300
  49.9 1.5 %write_out.1 = (bf16[8,512]{1,0:T(8,128)(2,1)}, bf16[512,768]{1,0:T(8,128)(2,1)}, bf16[512,768]{1,0:T(8,128)(2,1)}, bf16[768,512]{1,0:T(8,128)(2,1)}) custom-call(bf16[8,512]{1,0:T(8,128)(2,1)S(1)} %get-tuple-element.8.refs_0_, bf16[512,768]{1,0:T(8,128)(2,1)S(1)} %get-tuple-element.9.refs_1_, bf16[512,768]{1,0:T(8,128)(2,1)S(1)} %get-tuple-element.10.refs_2_, ...), custom_call_target="tpu_custom_call" | custom-call | tf_op jit(solution)/shard_map/write_out/pallas_call | solution.py:343

commit v4 on v3

--- a/solution.py
+++ b/solution.py
@@ -140,15 +140,24 @@
     order_tokens(ups_buf, ups_out)
 
     parts_z = []
+
+    def sum_pair(core, step, d):
+        k = lax.rem(z + d, n)
+        total = part_buf[core, xh * n + k] + x_recv[core, k].astype(F32)
+        if d:
+            z_send[k, core] = total.astype(BF16)
+            parts_z.append(
+                send(z_send.at[k, core], z_recv.at[d, core], zr_sem.at[step, d], z_peer(d))
+            )
+        else:
+            part_buf[core, row] = total
+
     first_x.wait_recv()
+    for d in x_order:
+        sum_pair(co, 0, d)
     for d, part_x in zip(x_order, parts_x):
-        k = lax.rem(z + d, n)
         part_x.wait_recv()
-        total = part_buf[:, xh * n + k] + x_recv[:, k].astype(F32)
-        if d:
-            z_send[k] = total.astype(BF16)
-            parts_z.append(send(z_send.at[k], z_recv.at[d], zr_sem.at[d], z_peer(d)))
-    part_buf[:, row] = total
+        sum_pair(1 - co, 1, d)
 
     wait_all(gu_z)
     gu_x = share(gu_buf.at[near_blocks], gu_sem.at[0], xh_peer)
@@ -170,7 +179,8 @@
     activations(xh * n)
 
     total = part_buf[:, row]
-    for d, part_z in zip(far_first(n)[::-1], parts_z[::-1]):
+    wait_all(parts_z[: n - 1])
+    for d, part_z in zip(far_first(n)[::-1], parts_z[: n - 2 : -1]):
         part_z.wait_recv()
         total = total + z_recv[d].astype(F32)
     hg_buf[row] = total.reshape(16, total.shape[-1]).astype(BF16)
@@ -290,7 +300,7 @@
     dma = pltpu.SemaphoreType.DMA
     hbm_spec = pl.BlockSpec(memory_space=pltpu.HBM)
     vmem_spec = pl.BlockSpec(memory_space=pltpu.VMEM)
-    n_sends = 8 * n + 2
+    n_sends = 9 * n + 1
     grad_shapes = (
         jax.ShapeDtypeStruct((8, d_block), BF16),
         jax.ShapeDtypeStruct((d_block, f_block), BF16),
@@ -330,7 +340,7 @@
             dma((7,)),
             dma((n_sends,)),
             dma((n,)), dma((n,)), dma((7,)),
-            dma((n + 1,)), dma((n,)), dma((n,)), dma((n,)), dma((2 * n,)), dma((2 * n,)), dma((n, 2)),
+            dma((n + 1,)), dma((2, n)), dma((n,)), dma((n,)), dma((2 * n,)), dma((2 * n,)), dma((n, 2)),
         ],
         compiler_params=pltpu.CompilerParams(
             collective_id=0, has_side_effects=True, vmem_limit_bytes=40 * 1024 * 1024

time: 51.6 us -> 51.1 us (level)
  no operation moved by 1% of the time
where the time goes in v4:
time: 51.1 us; the launch traced here: 50.9 us
  Pallas kernels  50.3 us (98%)
  between operations  0.64 us (1%)
    pallas_call x1, Pallas kernels, on_device(): pl.pallas_call(functools.partial(exchange, n, float(total) ** (-0.5)), na...  48.8 us
    pallas_call x1, Pallas kernels, on_device(): pl.pallas_call(write_out, name='write_out', in_specs=[vmem_spec] * 4, out...  1.46 us

profile of v4, /device:TPU:7, one launch (start us, length us, event | category | flops | bytes accessed | tf_op | source)
XLA Modules:
  0.0 50.9 jit_solution(8912124028377370672)
XLA Ops:
  0.6 48.8 %exchange.1 = (bf16[8,512]{1,0:T(8,128)(2,1)S(1)}, bf16[512,768]{1,0:T(8,128)(2,1)S(1)}, bf16[512,768]{1,0:T(8,128)(2,1)S(1)}, bf16[768,512]{1,0:T(8,128)(2,1)S(1)}) custom-call(bf16[8,512]{1,0:T(8,128)(2,1)} %ups.1, bf16[8,512]{1,0:T(8,128)(2,1)} %tok.1, bf16[16,768]{1,0:T(8,128)(2,1)} %gate.1, bf16[16,768]{1,0:T(8,128)(2,1)} %upre.1, ...), custom_call_target="tpu_custom_call" | custom-call | tf_op jit(solution)/shard_map/exchange/pallas_call | solution.py:310
  49.4 1.5 %write_out.1 = (bf16[8,512]{1,0:T(8,128)(2,1)}, bf16[512,768]{1,0:T(8,128)(2,1)}, bf16[512,768]{1,0:T(8,128)(2,1)}, bf16[768,512]{1,0:T(8,128)(2,1)}) custom-call(bf16[8,512]{1,0:T(8,128)(2,1)S(1)} %get-tuple-element.8.refs_0_, bf16[512,768]{1,0:T(8,128)(2,1)S(1)} %get-tuple-element.9.refs_1_, bf16[512,768]{1,0:T(8,128)(2,1)S(1)} %get-tuple-element.10.refs_2_, ...), custom_call_target="tpu_custom_call" | custom-call | tf_op jit(solution)/shard_map/write_out/pallas_call | solution.py:353
